TPU v7x, 32 devices: a whole 2x2x4 slice. The times are simulated.
32 devices in a mesh: row: 4 (over y, x), col: 2 (over core), depth: 4 (over z).
Axes of the slice: x: 2, y: 2, z: 4, core: 2. Of those that a mesh axis runs over, the one named last changes fastest.
Arguments:
- inputs: bfloat16 [512, 12288], P(('row', 'col'), 'depth'), may hold values from -90 to 90
- ln_gain: float32 [12288], P('depth'), may hold values from 0.25 to 1.75
- ln_shift: float32 [12288], P('depth'), may hold values from -3 to 3
- w_in: bfloat16 [12288, 24576], P('depth', ('row', 'col')), may hold values from -0.0546875 to 0.0546875
- b_in: float32 [24576], P(('row', 'col')), may hold values from -3 to 3
- w_out: bfloat16 [24576, 12288], P(('row', 'col'), 'depth'), may hold values from -0.0390625 to 0.0390625
- b_out: float32 [12288], P('depth'), may hold values from -3 to 3
- cotangent: bfloat16 [512, 12288], P(('row', 'col'), 'depth'), may hold values from -29 to 29
Outputs:
- output: bfloat16 [512, 12288], P(('row', 'col'), 'depth')
- grad_inputs: bfloat16 [512, 12288], P(('row', 'col'), 'depth')
- grad_w_in: bfloat16 [12288, 24576], P('depth', ('row', 'col'))
- grad_b_in: float32 [24576], P(('row', 'col'))
- grad_w_out: bfloat16 [24576, 12288], P(('row', 'col'), 'depth')
- grad_b_out: float32 [12288], P('depth')
- grad_gain: float32 [12288], P('depth')
- grad_shift: float32 [12288], P('depth')
All inputs are finite; a program needn't handle non-finite values.
Results may differ from a plain program's by a relative error of at most 0.0062.
Values may be sent and summed in bfloat16 or wider, within the bound.
A program may use at most 192 MiB of HBM per device.

v0:
```python
from functools import partial

import jax
import jax.numpy as jnp
from jax import lax
from jax.sharding import PartitionSpec as P

D = 12288


def gelu_back(pre_act, upstream):
    return jax.vjp(partial(jax.nn.gelu, approximate=True), pre_act)[1](upstream)[0]


def contract_rows(left, right):
    return lax.dot_general(
        left, right, (((0,), (0,)), ((), ())), preferred_element_type=jnp.float32
    )


def contract_cols(left, right):
    return lax.dot_general(
        left, right, (((1,), (1,)), ((), ())), preferred_element_type=jnp.float32
    )


def per_device(inputs, ln_gain, ln_shift, w_in, b_in, w_out, b_out, cotangent):
    wide_in = inputs.astype(jnp.float32)
    row_mean = lax.psum(jnp.sum(wide_in, axis=1, keepdims=True), "depth") / D
    centred = wide_in - row_mean
    row_var = lax.psum(jnp.sum(centred * centred, axis=1, keepdims=True), "depth") / D
    inv_std = 1.0 / jnp.sqrt(row_var + 1e-05)
    normed = centred * inv_std
    hidden_in = (normed * ln_gain + ln_shift).astype(jnp.bfloat16)
    hidden_all = lax.all_gather(hidden_in, ("row", "col"), axis=0, tiled=True)
    pre_act = (
        lax.psum_scatter(
            jnp.dot(hidden_all, w_in, preferred_element_type=jnp.float32),
            "depth",
            scatter_dimension=0,
            tiled=True,
        )
        + b_in
    )
    activated = jax.nn.gelu(pre_act, approximate=True).astype(jnp.bfloat16)
    active_all = lax.all_gather(activated, "depth", axis=0, tiled=True)
    projected = (
        lax.psum_scatter(
            jnp.dot(active_all, w_out, preferred_element_type=jnp.float32).astype(jnp.bfloat16),
            ("row", "col"),
            scatter_dimension=0,
            tiled=True,
        ).astype(jnp.float32)
        + b_out
    )
    output = (wide_in + projected).astype(jnp.bfloat16)
    grad_all = lax.all_gather(cotangent, ("row", "col"), axis=0, tiled=True)
    grad_w_out = contract_rows(active_all, grad_all).astype(jnp.bfloat16)
    act_grad = lax.psum_scatter(
        contract_cols(grad_all, w_out), "depth", scatter_dimension=0, tiled=True
    )
    pre_grad = gelu_back(pre_act, act_grad).astype(jnp.bfloat16)
    bias_part = jnp.sum(pre_grad.astype(jnp.float32), axis=0)
    pre_grad_all = lax.all_gather(pre_grad, "depth", axis=0, tiled=True)
    grad_w_in = contract_rows(hidden_all, pre_grad_all).astype(jnp.bfloat16)
    norm_grad = lax.psum_scatter(
        contract_cols(pre_grad_all, w_in), ("row", "col"), scatter_dimension=0, tiled=True
    )
    scaled_grad = norm_grad * ln_gain
    first_total, second_total, grad_b_in = lax.psum(
        (
            jnp.sum(scaled_grad, axis=1, keepdims=True),
            jnp.sum(scaled_grad * normed, axis=1, keepdims=True),
            bias_part,
        ),
        "depth",
    )
    grad_inputs = (
        cotangent.astype(jnp.float32)
        + inv_std * (scaled_grad - first_total / D - normed * (second_total / D))
    ).astype(jnp.bfloat16)
    grad_b_out, grad_gain, grad_shift = lax.psum(
        (
            jnp.sum(cotangent.astype(jnp.float32), axis=0),
            jnp.sum(norm_grad * normed, axis=0),
            jnp.sum(norm_grad, axis=0),
        ),
        ("row", "col"),
    )
    return (
        output,
        grad_inputs,
        grad_w_in,
        grad_b_in,
        grad_w_out,
        grad_b_out,
        grad_gain,
        grad_shift,
    )


def solution(mesh):
    return jax.shard_map(
        per_device,
        mesh=mesh,
        in_specs=(
            P(("row", "col"), "depth"),
            P("depth"),
            P("depth"),
            P("depth", ("row", "col")),
            P(("row", "col")),
            P(("row", "col"), "depth"),
            P("depth"),
            P(("row", "col"), "depth"),
        ),
        out_specs=(
            P(("row", "col"), "depth"),
            P(("row", "col"), "depth"),
            P("depth", ("row", "col")),
            P(("row", "col")),
            P(("row", "col"), "depth"),
            P("depth"),
            P("depth"),
            P("depth"),
        ),
        check_vma=False,
    )
```

profile of v0, /device:TPU:0, one launch (start us, length us, event | category | flops | bytes accessed | tf_op | source)
XLA Modules:
  0.0 607.4 jit_solution(4061698883704031266)
XLA Ops:
  8.4 13.5 %psum.56 = f32[64,1]{0,1:T(1,128)S(1)} all-reduce(f32[64,1]{0,1:T(1,128)S(1)} %bitcast.26), channel_id=1, replica_groups=mesh['row'=4,'col'=2,'depth'=4] {'depth'}, use_global_device_ids=true, to_apply=%region_1.0 | all-reduce | flops 64 | bytes 512 | tf_op jit(solution)/shard_map/psum | solution.py:29
  21.8 1.3 fusion.19
  23.1 8.4 %psum.57 = f32[64,1]{0,1:T(1,128)S(1)} all-reduce(f32[64,1]{0,1:T(1,128)S(1)} %bitcast.27), channel_id=1, replica_groups=mesh['row'=4,'col'=2,'depth'=4] {'depth'}, use_global_device_ids=true, to_apply=%region_3.0 | all-reduce | flops 64 | bytes 512 | tf_op jit(solution)/shard_map/psum | solution.py:31
  31.5 2.0 fusion.14
  34.3 31.3 %all-gather.5.cloned.1.call-done = bf16[512,3072]{1,0:T(8,128)(2,1)} async-done(((bf16[64,3072]{1,0:T(8,128)(2,1)}), bf16[512,3072]{1,0:T(8,128)(2,1)}) %all-gather.5.cloned.1.call-update) | async-done | bytes 3145744 | tf_op jit(solution)/shard_map/all_gather | solution.py:35
  65.6 16.3 %fusion.23 = f32[512,3072]{1,0:T(8,128)} fusion(bf16[512,3072]{1,0:T(8,128)(2,1)} %all-gather.5.cloned.1.call-done, bf16[3072,3072]{1,0:T(8,128)(2,1)} %param.11), kind=kOutput, calls=%fused_computation.39 | convolution fusion | flops 9663676416 | bytes 28311552 | tf_op jit(solution)/shard_map/dot_general | solution.py:38
  82.0 17.9 %all-gather.9.cloned.1.call-done = bf16[512,3072]{1,0:T(8,128)(2,1)} async-done(((bf16[64,3072]{1,0:T(8,128)(2,1)}), bf16[512,3072]{1,0:T(8,128)(2,1)}) %all-gather.9.cloned.1.call-update) | async-done | bytes 3145744 | tf_op jit(solution)/shard_map/all_gather | solution.py:57
  99.8 16.4 %fusion.24 = f32[512,3072]{1,0:T(8,128)} fusion(bf16[512,3072]{1,0:T(8,128)(2,1)} %all-gather.9.cloned.1.call-done, bf16[3072,3072]{1,0:T(8,128)(2,1)} %param.13), kind=kOutput, calls=%fused_computation.40 | convolution fusion | flops 9663676416 | bytes 28311552 | tf_op jit(solution)/shard_map/dot_general | solution.py:22
  116.3 97.2 %reduce-scatter.5.cloned.1.call-done = f32[128,3072]{1,0:T(8,128)} async-done(((f32[512,3072]{1,0:T(8,128)}), f32[128,3072]{1,0:T(8,128)}) %reduce-scatter.5.cloned.1.call-update) | async-done | bytes 1572880 | tf_op jit(solution)/shard_map/reduce_scatter | solution.py:37
  213.5 114.0 %reduce-scatter.9.cloned.1.call-done = f32[128,3072]{1,0:T(8,128)} async-done(((f32[512,3072]{1,0:T(8,128)}), f32[128,3072]{1,0:T(8,128)}) %reduce-scatter.9.cloned.1.call-update) | async-done | bytes 1572880 | tf_op jit(solution)/shard_map/reduce_scatter | solution.py:59
  327.5 4.2 convert_reduce_fusion
  332.6 63.4 %all-gather.11.cloned.1.call-done = bf16[512,3072]{1,0:T(8,128)(2,1)} async-done(((bf16[128,3072]{1,0:T(8,128)(2,1)}), bf16[512,3072]{1,0:T(8,128)(2,1)}) %all-gather.11.cloned.1.call-update) | async-done | bytes 3145744 | tf_op jit(solution)/shard_map/all_gather | solution.py:64
  396.0 16.4 %fusion.25 = f32[512,3072]{1,0:T(8,128)} fusion(bf16[512,3072]{1,0:T(8,128)(2,1)} %all-gather.11.cloned.1.call-done, bf16[3072,3072]{1,0:T(8,128)(2,1)} %param.11), kind=kOutput, calls=%fused_computation.41 | convolution fusion | flops 9663676416 | bytes 28311552 | tf_op jit(solution)/shard_map/dot_general | solution.py:22
  412.5 47.7 %all-gather.7.cloned.1.call-done = bf16[512,3072]{1,0:T(8,128)(2,1)} async-done(((bf16[128,3072]{1,0:T(8,128)(2,1)}), bf16[512,3072]{1,0:T(8,128)(2,1)}) %all-gather.7.cloned.1.call-update) | async-done | bytes 3145744 | tf_op jit(solution)/shard_map/all_gather | solution.py:46
  460.2 16.1 %convolution_convert_fusion.2 = bf16[512,3072]{1,0:T(8,128)(2,1)} fusion(bf16[512,3072]{1,0:T(8,128)(2,1)} %all-gather.7.cloned.1.call-done, bf16[3072,3072]{1,0:T(8,128)(2,1)} %param.13), kind=kOutput, calls=%fused_computation.2 | convolution fusion | flops 9665249280 | bytes 25165824 | tf_op jit(solution)/shard_map/dot_general | solution.py:49
  476.3 2.0 copy-done.5
  478.3 15.2 %convolution_convert_fusion.1 = bf16[3072,3072]{1,0:T(8,128)(2,1)} fusion(bf16[512,3072]{1,0:T(8,128)(2,1)S(1)} %copy-done.5, bf16[512,3072]{1,0:T(8,128)(2,1)} %all-gather.11.cloned.1.call-done), kind=kOutput, calls=%fused_computation.1 | convolution fusion | flops 9673113600 | bytes 25165824 | tf_op jit(solution)/shard_map/dot_general | solution.py:16
  493.6 13.3 %convolution_convert_fusion = bf16[3072,3072]{1,0:T(8,128)(2,1)} fusion(bf16[512,3072]{1,0:T(8,128)(2,1)S(1)} %copy-done.7, bf16[512,3072]{1,0:T(8,128)(2,1)S(1)} %copy-done.6), kind=kOutput, calls=%fused_computation | convolution fusion | flops 9673113600 | bytes 25165824 | tf_op jit(solution)/shard_map/dot_general | solution.py:16
  506.9 17.1 %reduce-scatter.11.cloned.1.call-done = f32[64,3072]{1,0:T(8,128)} async-done(((f32[512,3072]{1,0:T(8,128)}), f32[64,3072]{1,0:T(8,128)}) %reduce-scatter.11.cloned.1.call-update) | async-done | bytes 786448 | tf_op jit(solution)/shard_map/reduce_scatter | solution.py:66
  524.0 1.6 fusion.18
  525.6 19.3 %all-reduce.1 = (f32[64,1]{0,1:T(1,128)S(1)}, f32[64,1]{0,1:T(1,128)S(1)}, f32[3072]{0:T(1024)}) all-reduce(f32[64,1]{0,1:T(1,128)S(1)} %bitcast.24, f32[64,1]{0,1:T(1,128)S(1)} %bitcast.25, f32[3072]{0:T(1024)S(1)} %get-tuple-element.18), channel_id=1, replica_groups=mesh['row'=4,'col'=2,'depth'=4] {'depth'}, use_global_device_ids=true, to_apply=%region_11.0 | all-reduce | flops 3200 | bytes 25600 | tf_op jit(solution)/shard_map/psum | solution.py:70
  544.9 29.2 %reduce-scatter.7.cloned.1.call-done = bf16[64,3072]{1,0:T(8,128)(2,1)} async-done(((bf16[512,3072]{1,0:T(8,128)(2,1)}), bf16[64,3072]{1,0:T(8,128)(2,1)}) %reduce-scatter.7.cloned.1.call-update) | async-done | bytes 393232 | tf_op jit(solution)/shard_map/reduce_scatter | solution.py:48
  574.1 2.6 convert_reduce_fusion.2
  576.6 24.0 %all-reduce = (f32[3072]{0:T(1024)}, f32[3072]{0:T(1024)}, f32[3072]{0:T(1024)}) all-reduce(f32[3072]{0:T(1024)S(1)} %get-tuple-element.21, f32[3072]{0:T(1024)S(1)} %get-tuple-element.8, f32[3072]{0:T(1024)S(1)} %get-tuple-element.11), channel_id=1, replica_groups=mesh['row'=4,'col'=2,'depth'=4] {'row','col'}, use_global_device_ids=true, to_apply=%region_15.0 | all-reduce | flops 9216 | bytes 73728 | tf_op jit(solution)/shard_map/psum | solution.py:82
  (35 shorter events, 3.0 us)
Async XLA Ops:
  7.2 58.4 %all-gather.5.cloned.1.call-start = ((), (), s32[]{:S(2)}) async-start(), calls=%async_computation.4 | async-start | bytes 3538944 | tf_op jit(solution)/shard_map/all_gather | solution.py:35
  33.5 66.4 %all-gather.9.cloned.1.call-start = ((), (), s32[]{:S(2)}) async-start(), calls=%async_computation.8 | async-start | bytes 3538944 | tf_op jit(solution)/shard_map/all_gather | solution.py:57
  34.2 179.3 %reduce-scatter.5.cloned.1.call-start = ((), (), s32[]{:S(2)}) async-start(), calls=%async_computation.5 | async-start | bytes 7864320 | tf_op jit(solution)/shard_map/reduce_scatter | solution.py:37
  81.9 245.6 %reduce-scatter.9.cloned.1.call-start = ((), (), s32[]{:S(2)}) async-start(), calls=%async_computation.9 | async-start | bytes 7864320 | tf_op jit(solution)/shard_map/reduce_scatter | solution.py:59
  116.2 211.3 %copy-start.3 = (f32[3072]{0:T(1024)S(1)}, f32[3072]{0:T(1024)}, u32[]{:S(2)}) copy-start(f32[3072]{0:T(1024)} %param.12) | copy-start | bytes 36868
  116.2 279.7 %all-gather.11.cloned.1.call-start = ((), (), s32[]{:S(2)}) async-start(), calls=%async_computation.10 | async-start | bytes 3932160 | tf_op jit(solution)/shard_map/all_gather | solution.py:64
  331.8 128.4 %all-gather.7.cloned.1.call-start = ((), (), s32[]{:S(2)}) async-start(), calls=%async_computation.6 | async-start | bytes 3932160 | tf_op jit(solution)/shard_map/all_gather | solution.py:46
  332.4 191.6 %reduce-scatter.11.cloned.1.call-start = ((), (), s32[]{:S(2)}) async-start(), calls=%async_computation.11 | async-start | bytes 7077888 | tf_op jit(solution)/shard_map/reduce_scatter | solution.py:66
  412.4 161.6 %reduce-scatter.7.cloned.1.call-start = ((), (), s32[]{:S(2)}) async-start(), calls=%async_computation.7 | async-start | bytes 3538944 | tf_op jit(solution)/shard_map/reduce_scatter | solution.py:48
  476.3 2.0 copy-start.5
  478.3 15.2 %copy-start.6 = (bf16[512,3072]{1,0:T(8,128)(2,1)S(1)}, bf16[512,3072]{1,0:T(8,128)(2,1)}, u32[]{:S(2)}) copy-start(bf16[512,3072]{1,0:T(8,128)(2,1)} %all-gather.9.cloned.1.call-done) | copy-start | bytes 9437188
  478.3 15.2 %copy-start.7 = (bf16[512,3072]{1,0:T(8,128)(2,1)S(1)}, bf16[512,3072]{1,0:T(8,128)(2,1)}, u32[]{:S(2)}) copy-start(bf16[512,3072]{1,0:T(8,128)(2,1)} %all-gather.7.cloned.1.call-done) | copy-start | bytes 9437188
  493.5 30.5 %copy-start = (bf16[64,3072]{1,0:T(8,128)(2,1)S(1)}, bf16[64,3072]{1,0:T(8,128)(2,1)}, u32[]{:S(2)}) copy-start(bf16[64,3072]{1,0:T(8,128)(2,1)} %param.8) | copy-start | bytes 1179652
  493.5 30.5 %copy-start.2 = (f32[3072]{0:T(1024)S(1)}, f32[3072]{0:T(1024)}, u32[]{:S(2)}) copy-start(f32[3072]{0:T(1024)} %param.9) | copy-start | bytes 36868
  493.6 80.5 %copy-start.1 = (bf16[64,3072]{1,0:T(8,128)(2,1)S(1)}, bf16[64,3072]{1,0:T(8,128)(2,1)}, u32[]{:S(2)}) copy-start(bf16[64,3072]{1,0:T(8,128)(2,1)} %param.15) | copy-start | bytes 1179652
  493.6 80.5 %copy-start.4 = (f32[3072]{0:T(1024)S(1)}, f32[3072]{0:T(1024)}, u32[]{:S(2)}) copy-start(f32[3072]{0:T(1024)} %param.14) | copy-start | bytes 36868
Sparse Core Ops, SparseCore 0:
  33.6 31.9 all-gather.4
  67.5 32.3 all-gather.8
  102.7 110.7 reduce-scatter.4
  216.2 111.2 reduce-scatter.8
  331.9 64.0 all-gather.10
  398.0 62.1 all-gather.6
  463.6 60.3 reduce-scatter.10
  527.7 46.2 reduce-scatter.6
where the time goes:
time: 608 us; the launch traced here: 607 us
  waiting for transfers between devices  419 us (69%)
  matrix products  93.7 us (15%)
  blocking collectives  65.1 us (11%)
  between operations  14.2 us (2%)
  other arithmetic  12.8 us (2%)
    reduce_scatter x1, waiting for transfers between devices, per_device(): lax.psum_scatter(contract_cols(grad_all, w_out), 'depth', scatter_dimensi...  114 us
    reduce_scatter x1, waiting for transfers between devices, per_device(): lax.psum_scatter(jnp.dot(hidden_all, w_in, preferred_element_type=jnp.flo...  97.2 us
    all_gather x1, waiting for transfers between devices, per_device(): pre_grad_all = lax.all_gather(pre_grad, 'depth', axis=0, tiled=True)  63.4 us
    all_gather x1, waiting for transfers between devices, per_device(): active_all = lax.all_gather(activated, 'depth', axis=0, tiled=True)  47.7 us
    dot_general x2, matrix products, contract_cols(): lax.dot_general(left, right, (((1,), (1,)), ((), ())), preferred_element_...  32.8 us
    all_gather x1, waiting for transfers between devices, per_device(): hidden_all = lax.all_gather(hidden_in, ('row', 'col'), axis=0, tiled=True)  31.3 us
    reduce_scatter x1, waiting for transfers between devices, per_device(): lax.psum_scatter(jnp.dot(active_all, w_out, preferred_element_type=jnp.fl...  29.2 us
    dot_general x2, matrix products, contract_rows(): lax.dot_general(left, right, (((0,), (0,)), ((), ())), preferred_element_...  28.5 us
  transfers between devices with their start and end apart: 8, of which 8 were waited for; matrix products, arithmetic and copies ran while one was open for 16% of the time, Pallas kernels for 0%

commit v1 on v0

v1 whole, which is shorter than its diff:
```python
from functools import partial

import jax
import jax.numpy as jnp
from jax import lax
from jax.experimental import pallas as pl
from jax.experimental.pallas import tpu as pltpu
from jax.sharding import PartitionSpec as P

CHUNK = 256
HALVES = 2
SLOTS = 2
LAG = 1
MESH = pl.DeviceIdType.MESH


def gelu_both(pre, upstream):
    root = 0.7978845608028654
    square = pre * pre
    tanh = jnp.tanh(root * pre * (1.0 + 0.044715 * square))
    half = 0.5 * (1.0 + tanh)
    slope = half + 0.5 * pre * (1.0 - tanh * tanh) * (root * (1.0 + 0.134145 * square))
    return pre * half, upstream * slope


def contract_rows(left, right):
    return lax.dot_general(
        left, right, (((0,), (0,)), ((), ())), preferred_element_type=jnp.float32
    )


def contract_cols(left, right):
    return lax.dot_general(
        left, right, (((1,), (1,)), ((), ())), preferred_element_type=jnp.float32
    )


def line_kernel(
    n,
    hidden_hbm,
    grad_hbm,
    w_in,
    w_out,
    b_in,
    active_hbm,
    pre_grad_hbm,
    proj_hbm,
    norm_hbm,
    bias_ref,
    hidden,
    grad,
    own,
    from_left,
    from_right,
    to_right,
    to_left,
    proj,
    norm,
    early_in,
    early_out,
    late_in,
    late_out,
    result,
    load_sem,
    early_sem,
    late_sem,
    result_sem,
    send_right_sem,
    send_left_sem,
    recv_left_sem,
    recv_right_sem,
):
    rows, width = hidden.shape
    chunks = w_in.shape[1] // CHUNK
    sub = rows // HALVES
    me = lax.axis_index("depth")
    has_left, has_right = me > 0, me < n - 1
    left, right = jnp.maximum(me - 1, 0), jnp.minimum(me + 1, n - 1)
    tail = LAG * (n - 1)

    load_hidden = pltpu.make_async_copy(hidden_hbm, hidden, load_sem.at[0])
    load_grad = pltpu.make_async_copy(grad_hbm, grad, load_sem.at[1])
    load_grad.start()
    load_hidden.start()

    def columns(chunk):
        return pl.ds(pl.multiple_of(chunk * CHUNK, CHUNK), CHUNK)

    def weight_loads(chunk, to_in, to_out, sem):
        slot = lax.rem(chunk, 2)
        return (
            pltpu.make_async_copy(w_in.at[:, columns(chunk)], to_in.at[slot], sem.at[slot, 0]),
            pltpu.make_async_copy(w_out.at[columns(chunk), :], to_out.at[slot], sem.at[slot, 1]),
        )

    def start_early(chunk):
        for copy in weight_loads(chunk, early_in, early_out, early_sem):
            copy.start()

    def start_late(chunk):
        for copy in weight_loads(chunk, late_in, late_out, late_sem):
            copy.start()

    start_early(0)
    start_late(0)

    barrier = pltpu.get_barrier_semaphore()

    @pl.when(has_left)
    def _():
        pl.semaphore_signal(barrier, inc=1, device_id={"depth": left}, device_id_type=MESH)

    @pl.when(has_right)
    def _():
        pl.semaphore_signal(barrier, inc=1, device_id={"depth": right}, device_id_type=MESH)

    pl.semaphore_wait(barrier, has_left.astype(jnp.int32) + has_right.astype(jnp.int32))

    proj[...] = jnp.zeros_like(proj)
    norm[...] = jnp.zeros_like(norm)
    load_grad.wait()
    load_hidden.wait()

    def right_copy(chunk, kind, half):
        slot = lax.rem(chunk, SLOTS)
        return pltpu.make_async_remote_copy(
            src_ref=to_right.at[slot, kind, half],
            dst_ref=from_left.at[chunk, kind, half],
            send_sem=send_right_sem.at[slot, kind, half],
            recv_sem=recv_left_sem.at[chunk, kind, half],
            device_id={"depth": right},
            device_id_type=MESH,
        )

    def left_copy(chunk, kind, half):
        slot = lax.rem(chunk, SLOTS)
        return pltpu.make_async_remote_copy(
            src_ref=to_left.at[slot, kind, half],
            dst_ref=from_right.at[chunk, kind, half],
            send_sem=send_left_sem.at[slot, kind, half],
            recv_sem=recv_right_sem.at[chunk, kind, half],
            device_id={"depth": left},
            device_id_type=MESH,
        )

    def pass_on(chunk, kind, half, copy, incoming, outgoing, has_source, has_target):
        slot = lax.rem(chunk, SLOTS)

        @pl.when(has_source)
        def _():
            copy(chunk, kind, half).wait_recv()

        @pl.when(has_target)
        def _():
            @pl.when(chunk >= SLOTS)
            def _():
                copy(chunk - SLOTS, kind, half).wait_send()

            @pl.when(has_source)
            def _():
                outgoing[slot, kind, half] = (
                    own[chunk, kind, half] + incoming[chunk, kind, half].astype(jnp.float32)
                ).astype(jnp.bfloat16)

            @pl.when(jnp.logical_not(has_source))
            def _():
                outgoing[slot, kind, half] = own[chunk, kind, half].astype(jnp.bfloat16)

            copy(chunk, kind, half).start()

    def result_copies(chunk):
        slot = lax.rem(chunk, 2)
        return (
            pltpu.make_async_copy(
                result.at[slot, 0], active_hbm.at[:, columns(chunk)], result_sem.at[slot, 0]
            ),
            pltpu.make_async_copy(
                result.at[slot, 1], pre_grad_hbm.at[:, columns(chunk)], result_sem.at[slot, 1]
            ),
        )

    @pl.loop(0, chunks + tail)
    def _(step):
        @pl.when(step < chunks)
        def _():
            @pl.when(step + 1 < chunks)
            def _():
                start_early(step + 1)

            for copy in weight_loads(step, early_in, early_out, early_sem):
                copy.wait()
            slot = lax.rem(step, 2)
            for half in range(HALVES):
                own[step, 0, half] = contract_cols(
                    grad[half * sub : (half + 1) * sub, :], early_out[slot]
                )
            for half in range(HALVES):
                own[step, 1, half] = jnp.dot(
                    hidden[half * sub : (half + 1) * sub, :],
                    early_in[slot],
                    preferred_element_type=jnp.float32,
                )

        going_right = step - LAG * me
        going_left = step - LAG * (n - 1 - me)
        for kind in range(2):
            for half in range(HALVES):

                @pl.when(jnp.logical_and(going_right >= 0, going_right < chunks))
                def _():
                    pass_on(
                        going_right, kind, half, right_copy, from_left, to_right, has_left, has_right
                    )

                @pl.when(jnp.logical_and(going_left >= 0, going_left < chunks))
                def _():
                    pass_on(
                        going_left, kind, half, left_copy, from_right, to_left, has_right, has_left
                    )

        done = step - tail

        @pl.when(done >= 0)
        def _():
            slot = lax.rem(done, 2)

            @pl.when(done + 1 < chunks)
            def _():
                start_late(done + 1)

            @pl.when(done >= 2)
            def _():
                for copy in result_copies(done - 2):
                    copy.wait()

            for kind in range(2):
                for half in range(HALVES):

                    @pl.when(has_left)
                    def _():
                        own[done, kind, half] += from_left[done, kind, half].astype(jnp.float32)

                    @pl.when(has_right)
                    def _():
                        own[done, kind, half] += from_right[done, kind, half].astype(jnp.float32)

            bias = b_in[:, columns(done)]
            bias_grad = jnp.zeros((1, CHUNK), jnp.float32)
            for half in range(HALVES):
                active, pre_grad = gelu_both(own[done, 1, half] + bias, own[done, 0, half])
                pre_grad = pre_grad.astype(jnp.bfloat16)
                result[slot, 0, half * sub : (half + 1) * sub, :] = active.astype(jnp.bfloat16)
                result[slot, 1, half * sub : (half + 1) * sub, :] = pre_grad
                bias_grad += jnp.sum(pre_grad.astype(jnp.float32), axis=0, keepdims=True)
            bias_ref[:, columns(done)] = bias_grad
            for copy in result_copies(done):
                copy.start()
            for copy in weight_loads(done, late_in, late_out, late_sem):
                copy.wait()

            block = width // 2
            for part in range(2):
                span = slice(part * block, (part + 1) * block)
                proj[:, span] += jnp.dot(
                    result[slot, 0], late_out[slot, :, span], preferred_element_type=jnp.float32
                )
            for part in range(2):
                span = slice(part * block, (part + 1) * block)
                norm[:, span] += contract_cols(result[slot, 1], late_in[slot, span, :])

    hidden[...] = proj[...].astype(jnp.bfloat16)
    grad[...] = norm[...].astype(jnp.bfloat16)
    store_proj = pltpu.make_async_copy(hidden, proj_hbm, load_sem.at[0])
    store_norm = pltpu.make_async_copy(grad, norm_hbm, load_sem.at[1])
    store_proj.start()
    store_norm.start()
    for chunk in range(max(0, chunks - 2), chunks):
        for copy in result_copies(chunk):
            copy.wait()
    for chunk in range(max(0, chunks - SLOTS), chunks):
        for kind in range(2):
            for half in range(HALVES):

                @pl.when(has_right)
                def _():
                    right_copy(chunk, kind, half).wait_send()

                @pl.when(has_left)
                def _():
                    left_copy(chunk, kind, half).wait_send()

    store_proj.wait()
    store_norm.wait()


def line_call(n, hidden_all, grad_all, w_in, w_out, b_in):
    rows, width = hidden_all.shape
    local = w_in.shape[1]
    chunks = local // CHUNK
    sub = rows // HALVES
    anywhere = pl.BlockSpec(memory_space=pl.ANY)
    vmem = pl.BlockSpec(memory_space=pltpu.VMEM)
    bf16, f32 = jnp.bfloat16, jnp.float32
    parts = (2, HALVES)
    return pl.pallas_call(
        partial(line_kernel, n),
        out_shape=(
            jax.ShapeDtypeStruct((rows, local), bf16),
            jax.ShapeDtypeStruct((rows, local), bf16),
            jax.ShapeDtypeStruct((rows, width), bf16),
            jax.ShapeDtypeStruct((rows, width), bf16),
            jax.ShapeDtypeStruct((1, local), f32),
        ),
        in_specs=[anywhere] * 4 + [vmem],
        out_specs=(anywhere,) * 4 + (vmem,),
        scratch_shapes=[
            pltpu.VMEM((rows, width), bf16),
            pltpu.VMEM((rows, width), bf16),
            pltpu.VMEM((chunks, *parts, sub, CHUNK), f32),
            pltpu.VMEM((chunks, *parts, sub, CHUNK), bf16),
            pltpu.VMEM((chunks, *parts, sub, CHUNK), bf16),
            pltpu.VMEM((SLOTS, *parts, sub, CHUNK), bf16),
            pltpu.VMEM((SLOTS, *parts, sub, CHUNK), bf16),
            pltpu.VMEM((rows, width), f32),
            pltpu.VMEM((rows, width), f32),
            pltpu.VMEM((2, width, CHUNK), bf16),
            pltpu.VMEM((2, CHUNK, width), bf16),
            pltpu.VMEM((2, width, CHUNK), bf16),
            pltpu.VMEM((2, CHUNK, width), bf16),
            pltpu.VMEM((2, 2, rows, CHUNK), bf16),
            pltpu.SemaphoreType.DMA((2,)),
            pltpu.SemaphoreType.DMA((2, 2)),
            pltpu.SemaphoreType.DMA((2, 2)),
            pltpu.SemaphoreType.DMA((2, 2)),
            pltpu.SemaphoreType.DMA((SLOTS, *parts)),
            pltpu.SemaphoreType.DMA((SLOTS, *parts)),
            pltpu.SemaphoreType.DMA((chunks, *parts)),
            pltpu.SemaphoreType.DMA((chunks, *parts)),
        ],
        compiler_params=pltpu.CompilerParams(
            collective_id=0, has_side_effects=True, vmem_limit_bytes=62 * 2**20
        ),
        cost_estimate=pl.CostEstimate(
            flops=8 * rows * width * local,
            bytes_accessed=8 * width * local + 12 * rows * width,
            transcendentals=rows * local,
        ),
    )(hidden_all, grad_all, w_in, w_out, b_in)


def per_device(n, inputs, ln_gain, ln_shift, w_in, b_in, w_out, b_out, cotangent):
    width = inputs.shape[1]
    grad_all = lax.all_gather(cotangent, ("row", "col"), axis=0, tiled=True)
    wide_in = inputs.astype(jnp.float32)
    part_mean = jnp.mean(wide_in, axis=1, keepdims=True)
    part_square = jnp.sum((wide_in - part_mean) ** 2, axis=1, keepdims=True)
    stats = lax.all_gather(jnp.concatenate([part_mean, part_square], axis=1), "depth", axis=0)
    row_mean = jnp.mean(stats[:, :, :1], axis=0)
    row_var = (
        jnp.sum(stats[:, :, 1:], axis=0)
        + width * jnp.sum((stats[:, :, :1] - row_mean[None]) ** 2, axis=0)
    ) / (n * width)
    inv_std = 1.0 / jnp.sqrt(row_var + 1e-05)
    normed = (wide_in - row_mean) * inv_std
    hidden_in = (normed * ln_gain + ln_shift).astype(jnp.bfloat16)
    hidden_all = lax.all_gather(hidden_in, ("row", "col"), axis=0, tiled=True)
    active_all, pre_grad_all, proj_part, norm_part, bias_part = line_call(
        n, hidden_all, grad_all, w_in, w_out, b_in.reshape(1, -1)
    )
    projected = (
        lax.psum_scatter(proj_part, ("row", "col"), scatter_dimension=0, tiled=True).astype(
            jnp.float32
        )
        + b_out
    )
    output = (wide_in + projected).astype(jnp.bfloat16)
    norm_grad = lax.psum_scatter(
        norm_part, ("row", "col"), scatter_dimension=0, tiled=True
    ).astype(jnp.float32)
    grad_w_out = contract_rows(active_all, grad_all).astype(jnp.bfloat16)
    grad_w_in = contract_rows(hidden_all, pre_grad_all).astype(jnp.bfloat16)
    scaled_grad = norm_grad * ln_gain
    first_total, second_total, grad_b_in = lax.psum(
        (
            jnp.sum(scaled_grad, axis=1, keepdims=True),
            jnp.sum(scaled_grad * normed, axis=1, keepdims=True),
            bias_part[0] / n,
        ),
        "depth",
    )
    features = n * width
    grad_inputs = (
        cotangent.astype(jnp.float32)
        + inv_std * (scaled_grad - first_total / features - normed * (second_total / features))
    ).astype(jnp.bfloat16)
    grad_b_out, grad_gain, grad_shift = lax.psum(
        (
            jnp.sum(cotangent.astype(jnp.float32), axis=0),
            jnp.sum(norm_grad * normed, axis=0),
            jnp.sum(norm_grad, axis=0),
        ),
        ("row", "col"),
    )
    return (
        output,
        grad_inputs,
        grad_w_in,
        grad_b_in,
        grad_w_out,
        grad_b_out,
        grad_gain,
        grad_shift,
    )


def solution(mesh):
    return jax.shard_map(
        partial(per_device, mesh.shape["depth"]),
        mesh=mesh,
        in_specs=(
            P(("row", "col"), "depth"),
            P("depth"),
            P("depth"),
            P("depth", ("row", "col")),
            P(("row", "col")),
            P(("row", "col"), "depth"),
            P("depth"),
            P(("row", "col"), "depth"),
        ),
        out_specs=(
            P(("row", "col"), "depth"),
            P(("row", "col"), "depth"),
            P("depth", ("row", "col")),
            P(("row", "col")),
            P(("row", "col"), "depth"),
            P("depth"),
            P("depth"),
            P("depth"),
        ),
        check_vma=False,
    )
```

time: 608 us -> 378 us (0.62)
  waiting for transfers between devices: 419 us -> 100 us
  Pallas kernels: 0 us -> 169 us
  matrix products: 93.7 us -> 29.8 us
  blocking collectives: 65.1 us -> 56 us
    reduce_scatter x4 -> x2, waiting for transfers between devices: 258 us -> 44.8 us  [the longest x1 29.1 us: per_device(): lax.psum_scatter(proj_part, ('row', 'col'), scatter_dimension=0, tiled=True)]
    pallas_call x0 -> x1, Pallas kernels: none -> 169 us  [line_call(): pl.pallas_call(partial(line_kernel, n), out_shape=(jax.ShapeDtypeStruct((...]
    all_gather x2 -> x0, waiting for transfers between devices: 111 us -> none  [the longest x1 63.4 us: per_device(): pre_grad_all = lax.all_gather(pre_grad, 'depth', axis=0, tiled=True)]
    dot_general x4 -> x0, matrix products: 65.2 us -> none  [the longest x2 32.8 us: contract_cols(): lax.dot_general(left, right, (((1,), (1,)), ((), ())), preferred_element_...]
    psum x2 -> x0, blocking collectives: 21.8 us -> none  [the longest x1 13.5 us: per_device(): row_mean = lax.psum(jnp.sum(wide_in, axis=1, keepdims=True), 'depth') / D]
    all_gather x0 -> x1, blocking collectives: none -> 12.6 us  [per_device(): lax.all_gather(jnp.concatenate([part_mean, part_square], axis=1), 'depth'...]
  transfers between devices with their start and end apart: 8 -> 4, of which waited for: 8 -> 4; matrix products, arithmetic and copies ran while one was open for 16% -> 9% of each run, Pallas kernels for 0% -> 0%
where the time goes in v1:
time: 378 us
  Pallas kernels  169 us (45%)
  waiting for transfers between devices  100 us (26%)
  blocking collectives  56 us (15%)
  matrix products  29.8 us (8%)
  between operations  13.9 us (4%)
  other arithmetic  8.37 us (2%)
    pallas_call x1, Pallas kernels, line_call(): pl.pallas_call(partial(line_kernel, n), out_shape=(jax.ShapeDtypeStruct((...  169 us
    all_gather x1, waiting for transfers between devices, per_device(): hidden_all = lax.all_gather(hidden_in, ('row', 'col'), axis=0, tiled=True)  34.8 us
    dot_general x2, matrix products, contract_rows(): lax.dot_general(left, right, (((0,), (0,)), ((), ())), preferred_element_...  29.8 us
    reduce_scatter x1, waiting for transfers between devices, per_device(): lax.psum_scatter(proj_part, ('row', 'col'), scatter_dimension=0, tiled=True)  29.1 us
    psum x1, blocking collectives, per_device(): lax.psum((jnp.sum(cotangent.astype(jnp.float32), axis=0), jnp.sum(norm_gr...  24 us
    all_gather x1, waiting for transfers between devices, per_device(): grad_all = lax.all_gather(cotangent, ('row', 'col'), axis=0, tiled=True)  19.8 us
    psum x1, blocking collectives, per_device(): lax.psum((jnp.sum(scaled_grad, axis=1, keepdims=True), jnp.sum(scaled_gra...  19.3 us
    reduce_scatter x1, waiting for transfers between devices, per_device(): lax.psum_scatter(norm_part, ('row', 'col'), scatter_dimension=0, tiled=True)  15.7 us
  transfers between devices with their start and end apart: 4, of which 4 were waited for; matrix products, arithmetic and copies ran while one was open for 9% of the time, Pallas kernels for 0%

profile of v1, /device:TPU:0, one launch (start us, length us, event | category | flops | bytes accessed | tf_op | source)
XLA Modules:
  0.0 377.9 jit_solution(11124472112066738049)
XLA Ops:
  7.2 0.0 all-gather.7.cloned.1.call-start
  7.2 0.7 all-gather.7.cloned.1.call-update
  7.9 0.0 all-gather.5.cloned.1.call-start
  7.9 1.1 convert_reduce_fusion
  9.1 1.3 fusion.9
  10.4 12.6 %all-gather.1 = f32[4,64,2]{1,2,0:T(2,128)S(1)} all-gather(f32[1,64,2]{1,2,0:T(2,128)S(1)} %maximum_bitcast_fusion), channel_id=2, replica_groups=mesh['row'=4,'col'=2,'depth'=4] {'depth'}, dimensions={0}, use_global_device_ids=true | all-gather | bytes 2560 | tf_op jit(solution)/shard_map/all_gather | solution.py:357
  23.1 2.0 fusion.14
  25.1 0.0 all-gather.5.cloned.1.call-update
  25.1 0.0 reduce-scatter.5.cloned.1.call-start
  25.1 19.8 %all-gather.7.cloned.1.call-done.grad_hbm = bf16[512,3072]{1,0:T(8,128)(2,1)} async-done(((bf16[64,3072]{1,0:T(8,128)(2,1)}), bf16[512,3072]{1,0:T(8,128)(2,1)}) %all-gather.7.cloned.1.call-update) | async-done | bytes 3145744 | tf_op jit(solution)/shard_map/all_gather | solution.py:353
  44.9 34.8 %all-gather.5.cloned.1.call-done.hidden_hbm = bf16[512,3072]{1,0:T(8,128)(2,1)} async-done(((bf16[64,3072]{1,0:T(8,128)(2,1)}), bf16[512,3072]{1,0:T(8,128)(2,1)}) %all-gather.5.cloned.1.call-update) | async-done | bytes 3145744 | tf_op jit(solution)/shard_map/all_gather | solution.py:366
  79.7 169.0 %shard_map.143 = (bf16[512,3072]{1,0:T(8,128)(2,1)}, bf16[512,3072]{1,0:T(8,128)(2,1)}, bf16[512,3072]{1,0:T(8,128)(2,1)}, bf16[512,3072]{1,0:T(8,128)(2,1)}, f32[1,3072]{1,0:T(1,128)}) custom-call(bf16[512,3072]{1,0:T(8,128)(2,1)} %all-gather.5.cloned.1.call-done.hidden_hbm, bf16[512,3072]{1,0:T(8,128)(2,1)} %all-gather.7.cloned.1.call-done.grad_hbm, ...), custom_call_target="tpu_custom_call" | custom-call | flops 38654705664 | bytes 94371840 | tf_op jit(solution)/shard_map/pallas_call | solution.py:305
  248.7 0.0 reduce-scatter.5.cloned.1.call-update
  248.7 0.2 reduce-scatter.3.cloned.1.call-start
  249.0 0.3 reduce-scatter.3.cloned.1.call-update
  249.3 0.1 copy-done.4
  249.5 16.5 %convolution_convert_fusion.1 = bf16[3072,3072]{1,0:T(8,128)(2,1)} fusion(bf16[512,3072]{1,0:T(8,128)(2,1)} %all-gather.5.cloned.1.call-done.hidden_hbm, bf16[512,3072]{1,0:T(8,128)(2,1)} %get-tuple-element.15), kind=kOutput, calls=%fused_computation.1 | convolution fusion | flops 9673113600 | bytes 25165824 | tf_op jit(solution)/shard_map/dot_general | solution.py:27
  266.0 13.3 %convolution_convert_fusion = bf16[3072,3072]{1,0:T(8,128)(2,1)} fusion(bf16[512,3072]{1,0:T(8,128)(2,1)S(1)} %copy-done.6, bf16[512,3072]{1,0:T(8,128)(2,1)S(1)} %copy-done.5), kind=kOutput, calls=%fused_computation | convolution fusion | flops 9673113600 | bytes 25165824 | tf_op jit(solution)/shard_map/dot_general | solution.py:27
  279.3 15.7 %reduce-scatter.5.cloned.1.call-done = bf16[64,3072]{1,0:T(8,128)(2,1)} async-done(((bf16[512,3072]{1,0:T(8,128)(2,1)}), bf16[64,3072]{1,0:T(8,128)(2,1)}) %reduce-scatter.5.cloned.1.call-update) | async-done | bytes 393232 | tf_op jit(solution)/shard_map/reduce_scatter | solution.py:377
  295.0 1.4 fusion.7
  296.5 19.3 %all-reduce.1 = (f32[64,1]{0,1:T(1,128)S(1)}, f32[64,1]{0,1:T(1,128)S(1)}, f32[3072]{0:T(1024)}) all-reduce(f32[64,1]{0,1:T(1,128)S(1)} %bitcast.19, f32[64,1]{0,1:T(1,128)S(1)} %bitcast.20, f32[3072]{0:T(1024)S(1)} %bitcast.17), channel_id=1, replica_groups=mesh['row'=4,'col'=2,'depth'=4] {'depth'}, use_global_device_ids=true, to_apply=%region_10.0 | all-reduce | flops 3200 | bytes 25600 | tf_op jit(solution)/shard_map/psum | solution.py:383
  315.8 29.1 %reduce-scatter.3.cloned.1.call-done = bf16[64,3072]{1,0:T(8,128)(2,1)} async-done(((bf16[512,3072]{1,0:T(8,128)(2,1)}), bf16[64,3072]{1,0:T(8,128)(2,1)}) %reduce-scatter.3.cloned.1.call-update) | async-done | bytes 393232 | tf_op jit(solution)/shard_map/reduce_scatter | solution.py:371
  344.9 2.5 convert_reduce_fusion.2
  347.4 24.0 %all-reduce = (f32[3072]{0:T(1024)}, f32[3072]{0:T(1024)}, f32[3072]{0:T(1024)}) all-reduce(f32[3072]{0:T(1024)S(1)} %get-tuple-element.30, f32[3072]{0:T(1024)S(1)} %get-tuple-element.18, f32[3072]{0:T(1024)S(1)} %get-tuple-element.21), channel_id=1, replica_groups=mesh['row'=4,'col'=2,'depth'=4] {'row','col'}, use_global_device_ids=true, to_apply=%region_13.0 | all-reduce | flops 9216 | bytes 73728 | tf_op jit(solution)/shard_map/psum | solution.py:396
  (21 shorter events, 0.1 us)
Async XLA Ops:
  7.2 37.8 %all-gather.7.cloned.1.call-start = ((), (), s32[]{:S(2)}) async-start(), calls=%async_computation.3 | async-start | bytes 3538944 | tf_op jit(solution)/shard_map/all_gather | solution.py:353
  7.9 71.8 %all-gather.5.cloned.1.call-start = ((), (), s32[]{:S(2)}) async-start(), calls=%async_computation.2 | async-start | bytes 3538944 | tf_op jit(solution)/shard_map/all_gather | solution.py:366
  25.1 269.9 %reduce-scatter.5.cloned.1.call-start = ((), (), s32[]{:S(2)}) async-start(), calls=%async_computation.5 | async-start | bytes 3538944 | tf_op jit(solution)/shard_map/reduce_scatter | solution.py:377
  248.7 0.7 copy-start.4
  248.7 96.2 %reduce-scatter.3.cloned.1.call-start = ((), (), s32[]{:S(2)}) async-start(), calls=%async_computation.4 | async-start | bytes 3538944 | tf_op jit(solution)/shard_map/reduce_scatter | solution.py:371
  249.4 16.5 %copy-start.5 = (bf16[512,3072]{1,0:T(8,128)(2,1)S(1)}, bf16[512,3072]{1,0:T(8,128)(2,1)}, u32[]{:S(2)}) copy-start(bf16[512,3072]{1,0:T(8,128)(2,1)} %all-gather.7.cloned.1.call-done.grad_hbm) | copy-start | bytes 9437188
  249.4 16.5 %copy-start.6 = (bf16[512,3072]{1,0:T(8,128)(2,1)S(1)}, bf16[512,3072]{1,0:T(8,128)(2,1)}, u32[]{:S(2)}) copy-start(bf16[512,3072]{1,0:T(8,128)(2,1)} %get-tuple-element.17) | copy-start | bytes 9437188
  266.0 29.0 %copy-start = (bf16[64,3072]{1,0:T(8,128)(2,1)S(1)}, bf16[64,3072]{1,0:T(8,128)(2,1)}, u32[]{:S(2)}) copy-start(bf16[64,3072]{1,0:T(8,128)(2,1)} %param.8) | copy-start | bytes 1179652
  266.0 29.0 %copy-start.2 = (f32[3072]{0:T(1024)S(1)}, f32[3072]{0:T(1024)}, u32[]{:S(2)}) copy-start(f32[3072]{0:T(1024)} %param.9) | copy-start | bytes 36868
  266.0 78.9 %copy-start.1 = (bf16[64,3072]{1,0:T(8,128)(2,1)S(1)}, bf16[64,3072]{1,0:T(8,128)(2,1)}, u32[]{:S(2)}) copy-start(bf16[64,3072]{1,0:T(8,128)(2,1)} %param.15) | copy-start | bytes 1179652
  266.0 78.9 %copy-start.3 = (f32[3072]{0:T(1024)S(1)}, f32[3072]{0:T(1024)}, u32[]{:S(2)}) copy-start(f32[3072]{0:T(1024)} %param.14) | copy-start | bytes 36868
Sparse Core Ops, SparseCore 0:
  9.9 35.0 all-gather.6
  47.4 32.3 all-gather.4
  248.9 46.1 reduce-scatter.4
  298.6 46.2 reduce-scatter.2

commit v2 on v1

--- a/solution.py
+++ b/solution.py
@@ -37,16 +37,25 @@
 
 def line_kernel(
     n,
+    row_size,
+    col_size,
     hidden_hbm,
     grad_hbm,
     w_in,
     w_out,
     b_in,
+    b_out,
+    ln_gain,
+    inputs,
+    cotangent,
+    normed,
+    inv_std,
     active_hbm,
     pre_grad_hbm,
-    proj_hbm,
-    norm_hbm,
+    output_ref,
+    grad_inputs_ref,
     bias_ref,
+    sums_ref,
     hidden,
     grad,
     own,
@@ -69,14 +78,36 @@
     send_left_sem,
     recv_left_sem,
     recv_right_sem,
+    twin_recv,
+    chip_recv,
+    stats_send,
+    stats_recv,
+    bias_send,
+    bias_recv,
+    sums_send,
+    sums_recv,
+    twin_sems,
+    chip_sems,
+    stats_sems,
+    bias_sems,
+    sums_sems,
 ):
     rows, width = hidden.shape
     chunks = w_in.shape[1] // CHUNK
     sub = rows // HALVES
     me = lax.axis_index("depth")
+    row, col = lax.axis_index("row"), lax.axis_index("col")
+    group = row_size * col_size
+    chips = group // 2
+    per_row = col_size // 2
+    core = lax.rem(col, 2)
+    place = row * col_size + col
+    chip = row * per_row + col // 2
+    block_rows = rows // group
     has_left, has_right = me > 0, me < n - 1
     left, right = jnp.maximum(me - 1, 0), jnp.minimum(me + 1, n - 1)
     tail = LAG * (n - 1)
+    ring = own.shape[0]
 
     load_hidden = pltpu.make_async_copy(hidden_hbm, hidden, load_sem.at[0])
     load_grad = pltpu.make_async_copy(grad_hbm, grad, load_sem.at[1])
@@ -106,15 +137,22 @@
 
     barrier = pltpu.get_barrier_semaphore()
 
-    @pl.when(has_left)
-    def _():
-        pl.semaphore_signal(barrier, inc=1, device_id={"depth": left}, device_id_type=MESH)
-
-    @pl.when(has_right)
-    def _():
-        pl.semaphore_signal(barrier, inc=1, device_id={"depth": right}, device_id_type=MESH)
-
-    pl.semaphore_wait(barrier, has_left.astype(jnp.int32) + has_right.astype(jnp.int32))
+    def line_id(ahead):
+        return {"depth": lax.rem(me + ahead, n)}
+
+    def group_id(ahead):
+        other = lax.rem(place + ahead, group)
+        return {"row": other // col_size, "col": lax.rem(other, col_size)}
+
+    def chip_id(ahead):
+        other = lax.rem(chip + ahead, chips)
+        return {"row": other // per_row, "col": 2 * lax.rem(other, per_row) + core}
+
+    for ahead in range(1, n):
+        pl.semaphore_signal(barrier, inc=1, device_id=line_id(ahead), device_id_type=MESH)
+    for ahead in range(1, group):
+        pl.semaphore_signal(barrier, inc=1, device_id=group_id(ahead), device_id_type=MESH)
+    pl.semaphore_wait(barrier, n - 1 + group - 1)
 
     proj[...] = jnp.zeros_like(proj)
     norm[...] = jnp.zeros_like(norm)
@@ -159,12 +197,12 @@
             @pl.when(has_source)
             def _():
                 outgoing[slot, kind, half] = (
-                    own[chunk, kind, half] + incoming[chunk, kind, half].astype(jnp.float32)
+                    own[lax.rem(chunk, ring), kind, half] + incoming[chunk, kind, half].astype(jnp.float32)
                 ).astype(jnp.bfloat16)
 
             @pl.when(jnp.logical_not(has_source))
             def _():
-                outgoing[slot, kind, half] = own[chunk, kind, half].astype(jnp.bfloat16)
+                outgoing[slot, kind, half] = own[lax.rem(chunk, ring), kind, half].astype(jnp.bfloat16)
 
             copy(chunk, kind, half).start()
 
@@ -191,11 +229,11 @@
                 copy.wait()
             slot = lax.rem(step, 2)
             for half in range(HALVES):
-                own[step, 0, half] = contract_cols(
+                own[lax.rem(step, ring), 0, half] = contract_cols(
                     grad[half * sub : (half + 1) * sub, :], early_out[slot]
                 )
             for half in range(HALVES):
-                own[step, 1, half] = jnp.dot(
+                own[lax.rem(step, ring), 1, half] = jnp.dot(
                     hidden[half * sub : (half + 1) * sub, :],
                     early_in[slot],
                     preferred_element_type=jnp.float32,
@@ -238,16 +276,16 @@
 
                     @pl.when(has_left)
                     def _():
-                        own[done, kind, half] += from_left[done, kind, half].astype(jnp.float32)
+                        own[lax.rem(done, ring), kind, half] += from_left[done, kind, half].astype(jnp.float32)
 
                     @pl.when(has_right)
                     def _():
-                        own[done, kind, half] += from_right[done, kind, half].astype(jnp.float32)
+                        own[lax.rem(done, ring), kind, half] += from_right[done, kind, half].astype(jnp.float32)
 
             bias = b_in[:, columns(done)]
             bias_grad = jnp.zeros((1, CHUNK), jnp.float32)
             for half in range(HALVES):
-                active, pre_grad = gelu_both(own[done, 1, half] + bias, own[done, 0, half])
+                active, pre_grad = gelu_both(own[lax.rem(done, ring), 1, half] + bias, own[lax.rem(done, ring), 0, half])
                 pre_grad = pre_grad.astype(jnp.bfloat16)
                 result[slot, 0, half * sub : (half + 1) * sub, :] = active.astype(jnp.bfloat16)
                 result[slot, 1, half * sub : (half + 1) * sub, :] = pre_grad
@@ -268,12 +306,131 @@
                 span = slice(part * block, (part + 1) * block)
                 norm[:, span] += contract_cols(result[slot, 1], late_in[slot, span, :])
 
-    hidden[...] = proj[...].astype(jnp.bfloat16)
-    grad[...] = norm[...].astype(jnp.bfloat16)
-    store_proj = pltpu.make_async_copy(hidden, proj_hbm, load_sem.at[0])
-    store_norm = pltpu.make_async_copy(grad, norm_hbm, load_sem.at[1])
-    store_proj.start()
-    store_norm.start()
+    def remote(src, dst, sems, at, device):
+        return pltpu.make_async_remote_copy(
+            src_ref=src,
+            dst_ref=dst,
+            send_sem=sems.at[0, at],
+            recv_sem=sems.at[1, at],
+            device_id=device,
+            device_id_type=MESH,
+        )
+
+    bias_send[...] = bias_ref[...]
+    bias_copies = [
+        remote(bias_send, bias_recv.at[ahead - 1], bias_sems, ahead - 1, line_id(ahead))
+        for ahead in range(1, n)
+    ]
+    for copy in bias_copies:
+        copy.start()
+
+    def rows_of(chip_at, core_at):
+        at = (chip_at * 2 + core_at) * block_rows
+        return pl.ds(pl.multiple_of(at, block_rows), block_rows)
+
+    totals, stages = (norm, proj), (grad, hidden)
+    twin_rows = chips * block_rows
+    twin_copies = []
+    for at in range(2):
+        for which in range(chips):
+            stages[at][which * block_rows : (which + 1) * block_rows, :] = totals[at][
+                rows_of(which, 1 - core), :
+            ].astype(jnp.bfloat16)
+        copy = remote(
+            stages[at].at[:twin_rows],
+            twin_recv.at[at],
+            twin_sems,
+            at,
+            {"col": col + 1 - 2 * core},
+        )
+        copy.start()
+        twin_copies.append(copy)
+
+    def both_cores(at, which):
+        from_twin = twin_recv[at, pl.ds(pl.multiple_of(which * block_rows, block_rows), block_rows), :]
+        return totals[at][rows_of(which, core), :] + from_twin.astype(jnp.float32)
+
+    chip_copies = []
+    for at in range(2):
+        twin_copies[at].wait_recv()
+        of_array = []
+        for ahead in range(1, chips):
+            spot = slice(twin_rows + (ahead - 1) * block_rows, twin_rows + ahead * block_rows)
+            stages[at][spot, :] = both_cores(at, lax.rem(chip + ahead, chips)).astype(jnp.bfloat16)
+            copy = remote(
+                stages[at].at[spot],
+                chip_recv.at[at, ahead - 1],
+                chip_sems,
+                at * (chips - 1) + ahead - 1,
+                chip_id(ahead),
+            )
+            copy.start()
+            of_array.append(copy)
+        chip_copies.append(of_array)
+
+    def summed(at):
+        value = both_cores(at, chip)
+        for ahead in range(1, chips):
+            chip_copies[at][ahead - 1].wait_recv()
+            value += chip_recv[at, ahead - 1].astype(jnp.float32)
+        return value
+
+    mine = pl.ds(0, block_rows)
+    norm_grad = summed(0)
+    sums_send[0] = jnp.sum(norm_grad * normed[...], axis=0, keepdims=True)
+    sums_send[1] = jnp.sum(norm_grad, axis=0, keepdims=True)
+    sums_copies = [
+        remote(sums_send, sums_recv.at[ahead - 1], sums_sems, ahead - 1, group_id(ahead))
+        for ahead in range(1, group)
+    ]
+    for copy in sums_copies:
+        copy.start()
+    scaled = norm_grad * ln_gain[...]
+    first = jnp.sum(scaled, axis=1, keepdims=True)
+    second = jnp.sum(scaled * normed[...], axis=1, keepdims=True)
+    lane = lax.broadcasted_iota(jnp.int32, stats_send.shape, 1)
+    stats_send[...] = jnp.where(lane == 0, first, second)
+    stats_copies = [
+        remote(stats_send, stats_recv.at[ahead - 1], stats_sems, ahead - 1, line_id(ahead))
+        for ahead in range(1, n)
+    ]
+    for copy in stats_copies:
+        copy.start()
+    norm[mine, :] = scaled
+
+    output_ref[...] = (inputs[...].astype(jnp.float32) + (summed(1) + b_out[...])).astype(
+        jnp.bfloat16
+    )
+
+    stats = stats_send[...]
+    for ahead in range(1, n):
+        stats_copies[ahead - 1].wait_recv()
+        stats += stats_recv[ahead - 1]
+    features = n * width
+    grad_inputs_ref[...] = (
+        cotangent[...].astype(jnp.float32)
+        + inv_std[...]
+        * (norm[mine, :] - stats[:, :1] / features - normed[...] * (stats[:, 1:2] / features))
+    ).astype(jnp.bfloat16)
+    sums = sums_send[...]
+    for ahead in range(1, group):
+        sums_copies[ahead - 1].wait_recv()
+        sums += sums_recv[ahead - 1]
+    sums_ref[...] = sums
+    bias_total = bias_send[...]
+    for ahead in range(1, n):
+        bias_copies[ahead - 1].wait_recv()
+        bias_total += bias_recv[ahead - 1]
+    bias_ref[...] = bias_total / n
+    for copy in [
+        *twin_copies,
+        *chip_copies[0],
+        *chip_copies[1],
+        *stats_copies,
+        *sums_copies,
+        *bias_copies,
+    ]:
+        copy.wait_send()
     for chunk in range(max(0, chunks - 2), chunks):
         for copy in result_copies(chunk):
             copy.wait()
@@ -289,12 +446,14 @@
                 def _():
                     left_copy(chunk, kind, half).wait_send()
 
-    store_proj.wait()
-    store_norm.wait()
-
-
-def line_call(n, hidden_all, grad_all, w_in, w_out, b_in):
+
+def line_call(
+    n, row_size, col_size, hidden_all, grad_all, w_in, w_out, b_in, b_out, ln_gain, inputs, cotangent, normed, inv_std
+):
     rows, width = hidden_all.shape
+    group = row_size * col_size
+    chips = group // 2
+    block_rows = rows // group
     local = w_in.shape[1]
     chunks = local // CHUNK
     sub = rows // HALVES
@@ -303,20 +462,21 @@
     bf16, f32 = jnp.bfloat16, jnp.float32
     parts = (2, HALVES)
     return pl.pallas_call(
-        partial(line_kernel, n),
+        partial(line_kernel, n, row_size, col_size),
         out_shape=(
             jax.ShapeDtypeStruct((rows, local), bf16),
             jax.ShapeDtypeStruct((rows, local), bf16),
-            jax.ShapeDtypeStruct((rows, width), bf16),
-            jax.ShapeDtypeStruct((rows, width), bf16),
+            jax.ShapeDtypeStruct((block_rows, width), bf16),
+            jax.ShapeDtypeStruct((block_rows, width), bf16),
             jax.ShapeDtypeStruct((1, local), f32),
+            jax.ShapeDtypeStruct((2, 1, width), f32),
         ),
-        in_specs=[anywhere] * 4 + [vmem],
-        out_specs=(anywhere,) * 4 + (vmem,),
+        in_specs=[anywhere] * 4 + [vmem] * 7,
+        out_specs=(anywhere,) * 2 + (vmem,) * 4,
         scratch_shapes=[
             pltpu.VMEM((rows, width), bf16),
             pltpu.VMEM((rows, width), bf16),
-            pltpu.VMEM((chunks, *parts, sub, CHUNK), f32),
+            pltpu.VMEM((min(chunks, LAG * (n - 1) + 1), *parts, sub, CHUNK), f32),
             pltpu.VMEM((chunks, *parts, sub, CHUNK), bf16),
             pltpu.VMEM((chunks, *parts, sub, CHUNK), bf16),
             pltpu.VMEM((SLOTS, *parts, sub, CHUNK), bf16),
@@ -336,6 +496,19 @@
             pltpu.SemaphoreType.DMA((SLOTS, *parts)),
             pltpu.SemaphoreType.DMA((chunks, *parts)),
             pltpu.SemaphoreType.DMA((chunks, *parts)),
+            pltpu.VMEM((2, chips * block_rows, width), bf16),
+            pltpu.VMEM((2, chips - 1, block_rows, width), bf16),
+            pltpu.VMEM((block_rows, 128), f32),
+            pltpu.VMEM((n - 1, block_rows, 128), f32),
+            pltpu.VMEM((1, local), f32),
+            pltpu.VMEM((n - 1, 1, local), f32),
+            pltpu.VMEM((2, 1, width), f32),
+            pltpu.VMEM((group - 1, 2, 1, width), f32),
+            pltpu.SemaphoreType.DMA((2, 2)),
+            pltpu.SemaphoreType.DMA((2, 2 * (chips - 1))),
+            pltpu.SemaphoreType.DMA((2, n - 1)),
+            pltpu.SemaphoreType.DMA((2, n - 1)),
+            pltpu.SemaphoreType.DMA((2, group - 1)),
         ],
         compiler_params=pltpu.CompilerParams(
             collective_id=0, has_side_effects=True, vmem_limit_bytes=62 * 2**20
@@ -345,10 +518,12 @@
             bytes_accessed=8 * width * local + 12 * rows * width,
             transcendentals=rows * local,
         ),
-    )(hidden_all, grad_all, w_in, w_out, b_in)
-
-
-def per_device(n, inputs, ln_gain, ln_shift, w_in, b_in, w_out, b_out, cotangent):
+    )(
+        hidden_all, grad_all, w_in, w_out, b_in, b_out, ln_gain, inputs, cotangent, normed, inv_std
+    )
+
+
+def per_device(n, row_size, col_size, inputs, ln_gain, ln_shift, w_in, b_in, w_out, b_out, cotangent):
     width = inputs.shape[1]
     grad_all = lax.all_gather(cotangent, ("row", "col"), axis=0, tiled=True)
     wide_in = inputs.astype(jnp.float32)
@@ -364,43 +539,27 @@
     normed = (wide_in - row_mean) * inv_std
     hidden_in = (normed * ln_gain + ln_shift).astype(jnp.bfloat16)
     hidden_all = lax.all_gather(hidden_in, ("row", "col"), axis=0, tiled=True)
-    active_all, pre_grad_all, proj_part, norm_part, bias_part = line_call(
-        n, hidden_all, grad_all, w_in, w_out, b_in.reshape(1, -1)
+    active_all, pre_grad_all, output, grad_inputs, grad_b_in, sums = line_call(
+        n,
+        row_size,
+        col_size,
+        hidden_all,
+        grad_all,
+        w_in,
+        w_out,
+        b_in.reshape(1, -1),
+        b_out.reshape(1, -1),
+        ln_gain.reshape(1, -1),
+        inputs,
+        cotangent,
+        normed,
+        inv_std,
     )
-    projected = (
-        lax.psum_scatter(proj_part, ("row", "col"), scatter_dimension=0, tiled=True).astype(
-            jnp.float32
-        )
-        + b_out
-    )
-    output = (wide_in + projected).astype(jnp.bfloat16)
-    norm_grad = lax.psum_scatter(
-        norm_part, ("row", "col"), scatter_dimension=0, tiled=True
-    ).astype(jnp.float32)
     grad_w_out = contract_rows(active_all, grad_all).astype(jnp.bfloat16)
     grad_w_in = contract_rows(hidden_all, pre_grad_all).astype(jnp.bfloat16)
-    scaled_grad = norm_grad * ln_gain
-    first_total, second_total, grad_b_in = lax.psum(
-        (
-            jnp.sum(scaled_grad, axis=1, keepdims=True),
-            jnp.sum(scaled_grad * normed, axis=1, keepdims=True),
-            bias_part[0] / n,
-        ),
-        "depth",
-    )
-    features = n * width
-    grad_inputs = (
-        cotangent.astype(jnp.float32)
-        + inv_std * (scaled_grad - first_total / features - normed * (second_total / features))
-    ).astype(jnp.bfloat16)
-    grad_b_out, grad_gain, grad_shift = lax.psum(
-        (
-            jnp.sum(cotangent.astype(jnp.float32), axis=0),
-            jnp.sum(norm_grad * normed, axis=0),
-            jnp.sum(norm_grad, axis=0),
-        ),
-        ("row", "col"),
-    )
+    grad_b_out = jnp.sum(grad_all.astype(jnp.float32), axis=0)
+    grad_gain, grad_shift = sums[0, 0], sums[1, 0]
+    grad_b_in = grad_b_in[0]
     return (
         output,
         grad_inputs,
@@ -415,7 +574,7 @@
 
 def solution(mesh):
     return jax.shard_map(
-        partial(per_device, mesh.shape["depth"]),
+        partial(per_device, mesh.shape["depth"], mesh.shape["row"], mesh.shape["col"]),
         mesh=mesh,
         in_specs=(
             P(("row", "col"), "depth"),

time: 378 us -> 340 us (0.90)
  blocking collectives: 56 us -> 12.6 us
  Pallas kernels: 169 us -> 208 us
  waiting for transfers between devices: 100 us -> 64.2 us
  local copies, waits for them, and re-layouts: 0.13 us -> 4.31 us
    reduce_scatter x2 -> x0, waiting for transfers between devices: 44.8 us -> none  [the longest x1 29.1 us: per_device(): lax.psum_scatter(proj_part, ('row', 'col'), scatter_dimension=0, tiled=True)]
    psum x2 -> x0, blocking collectives: 43.3 us -> none  [the longest x1 24 us: per_device(): lax.psum((jnp.sum(cotangent.astype(jnp.float32), axis=0), jnp.sum(norm_gr...]
    pallas_call x1, Pallas kernels: 169 us -> 208 us  [line_call(): pl.pallas_call(partial(line_kernel, n, row_size, col_size), out_shape=(ja...]
    all_gather x1, waiting for transfers between devices: 19.8 us -> 34.2 us  [per_device(): grad_all = lax.all_gather(cotangent, ('row', 'col'), axis=0, tiled=True)]
    all_gather x1, waiting for transfers between devices: 34.8 us -> 29.2 us  [per_device(): hidden_all = lax.all_gather(hidden_in, ('row', 'col'), axis=0, tiled=True)]
  transfers between devices with their start and end apart: 4 -> 2, of which waited for: 4 -> 2; matrix products, arithmetic and copies ran while one was open for 9% -> 0% of each run, Pallas kernels for 0% -> 0%
where the time goes in v2:
time: 340 us; the launch traced here: 339 us
  Pallas kernels  208 us (61%)
  waiting for transfers between devices  64.2 us (19%)
  matrix products  28.7 us (8%)
  between operations  14.1 us (4%)
  blocking collectives  12.6 us (4%)
  other arithmetic  7.85 us (2%)
  local copies, waits for them, and re-layouts  4.31 us (1%)
    pallas_call x1, Pallas kernels, line_call(): pl.pallas_call(partial(line_kernel, n, row_size, col_size), out_shape=(ja...  208 us
    all_gather x1, waiting for transfers between devices, per_device(): grad_all = lax.all_gather(cotangent, ('row', 'col'), axis=0, tiled=True)  34.2 us
    all_gather x1, waiting for transfers between devices, per_device(): hidden_all = lax.all_gather(hidden_in, ('row', 'col'), axis=0, tiled=True)  29.2 us
    dot_general x2, matrix products, contract_rows(): lax.dot_general(left, right, (((0,), (0,)), ((), ())), preferred_element_...  28.7 us
    all_gather x1, blocking collectives, per_device(): lax.all_gather(jnp.concatenate([part_mean, part_square], axis=1), 'depth'...  12.6 us
  transfers between devices with their start and end apart: 2, of which 2 were waited for; matrix products, arithmetic and copies ran while one was open for 0% of the time, Pallas kernels for 0%

profile of v2, /device:TPU:0, one launch (start us, length us, event | category | flops | bytes accessed | tf_op | source)
XLA Modules:
  0.0 339.5 jit_solution(13957870761968161388)
XLA Ops:
  7.2 0.0 all-gather.5.cloned.1.call-start
  7.2 1.1 convert_reduce_fusion.1
  8.4 1.3 fusion.1
  9.7 12.6 %all-gather.1 = f32[4,64,2]{1,2,0:T(2,128)S(1)} all-gather(f32[1,64,2]{1,2,0:T(2,128)S(1)} %maximum_bitcast_fusion), channel_id=2, replica_groups=mesh['row'=4,'col'=2,'depth'=4] {'depth'}, dimensions={0}, use_global_device_ids=true | all-gather | bytes 2560 | tf_op jit(solution)/shard_map/all_gather | solution.py:532
  22.3 2.2 fusion.2
  24.6 0.0 all-gather.5.cloned.1.call-update
  24.6 0.0 all-gather.7.cloned.1.call-start
  24.7 0.7 all-gather.7.cloned.1.call-update
  25.4 0.7 copy.17.inv_std
  26.1 29.2 %all-gather.5.cloned.1.call-done.hidden_hbm = bf16[512,3072]{1,0:T(8,128)(2,1)} async-done(((bf16[64,3072]{1,0:T(8,128)(2,1)}), bf16[512,3072]{1,0:T(8,128)(2,1)}) %all-gather.5.cloned.1.call-update) | async-done | bytes 3145744 | tf_op jit(solution)/shard_map/all_gather | solution.py:541
  55.3 34.2 %all-gather.7.cloned.1.call-done.grad_hbm = bf16[512,3072]{1,0:T(8,128)(2,1)} async-done(((bf16[64,3072]{1,0:T(8,128)(2,1)}), bf16[512,3072]{1,0:T(8,128)(2,1)}) %all-gather.7.cloned.1.call-update) | async-done | bytes 3145744 | tf_op jit(solution)/shard_map/all_gather | solution.py:528
  89.5 207.6 %shard_map.143 = (bf16[512,3072]{1,0:T(8,128)(2,1)}, bf16[512,3072]{1,0:T(8,128)(2,1)}, bf16[64,3072]{1,0:T(8,128)(2,1)}, bf16[64,3072]{1,0:T(8,128)(2,1)}, f32[1,3072]{1,0:T(1,128)}, /*index=5*/f32[2,1,3072]{2,1,0:T(1,128)}) custom-call(bf16[512,3072]{1,0:T(8,128)(2,1)} %all-gather.5.cloned.1.call-done.hidden_hbm, ...), custom_call_target="tpu_custom_call" | custom-call | flops 38654705664 | bytes 94371840 | tf_op jit(solution)/shard_map/pallas_call | solution.py:464
  297.1 0.0 copy-start.4
  297.1 1.5 fusion.4
  298.6 3.1 convert_reduce_fusion
  301.7 0.0 copy-done.4
  301.8 15.2 %convolution_convert_fusion.1 = bf16[3072,3072]{1,0:T(8,128)(2,1)} fusion(bf16[512,3072]{1,0:T(8,128)(2,1)S(1)} %copy-done.4, bf16[512,3072]{1,0:T(8,128)(2,1)} %get-tuple-element.16), kind=kOutput, calls=%fused_computation.1 | convolution fusion | flops 9673113600 | bytes 25165824 | tf_op jit(solution)/shard_map/dot_general | solution.py:27
  317.0 0.0 copy-done
  317.0 0.0 copy-done.5
  317.0 13.5 %convolution_convert_fusion = bf16[3072,3072]{1,0:T(8,128)(2,1)} fusion(bf16[512,3072]{1,0:T(8,128)(2,1)S(1)} %copy-done.5, bf16[512,3072]{1,0:T(8,128)(2,1)S(1)} %copy-done), kind=kOutput, calls=%fused_computation | convolution fusion | flops 9673113600 | bytes 25165824 | tf_op jit(solution)/shard_map/dot_general | solution.py:27
  330.5 0.7 copy.21
  331.3 0.0 copy-done.1
  331.3 0.7 copy.22
  332.0 0.6 copy.23
  (13 shorter events, 0.1 us)
Async XLA Ops:
  7.2 48.1 %all-gather.5.cloned.1.call-start = ((), (), s32[]{:S(2)}) async-start(), calls=%async_computation | async-start | bytes 3538944 | tf_op jit(solution)/shard_map/all_gather | solution.py:541
  24.6 64.9 %all-gather.7.cloned.1.call-start = ((), (), s32[]{:S(2)}) async-start(), calls=%async_computation.1 | async-start | bytes 3538944 | tf_op jit(solution)/shard_map/all_gather | solution.py:528
  297.1 4.6 %copy-start.4 = (bf16[512,3072]{1,0:T(8,128)(2,1)S(1)}, bf16[512,3072]{1,0:T(8,128)(2,1)}, u32[]{:S(2)}) copy-start(bf16[512,3072]{1,0:T(8,128)(2,1)} %all-gather.5.cloned.1.call-done.hidden_hbm) | copy-start | bytes 9437188
  301.7 15.2 %copy-start = (bf16[512,3072]{1,0:T(8,128)(2,1)S(1)}, bf16[512,3072]{1,0:T(8,128)(2,1)}, u32[]{:S(2)}) copy-start(bf16[512,3072]{1,0:T(8,128)(2,1)} %all-gather.7.cloned.1.call-done.grad_hbm) | copy-start | bytes 9437188
  301.7 15.2 %copy-start.5 = (bf16[512,3072]{1,0:T(8,128)(2,1)S(1)}, bf16[512,3072]{1,0:T(8,128)(2,1)}, u32[]{:S(2)}) copy-start(bf16[512,3072]{1,0:T(8,128)(2,1)} %get-tuple-element.18) | copy-start | bytes 9437188
  317.0 13.5 %copy-start.2 = (bf16[64,3072]{1,0:T(8,128)(2,1)S(1)}, bf16[64,3072]{1,0:T(8,128)(2,1)}, u32[]{:S(2)}) copy-start(bf16[64,3072]{1,0:T(8,128)(2,1)} %get-tuple-element.36) | copy-start | bytes 1179652
  317.0 14.3 %copy-start.1 = (bf16[64,3072]{1,0:T(8,128)(2,1)S(1)}, bf16[64,3072]{1,0:T(8,128)(2,1)}, u32[]{:S(2)}) copy-start(bf16[64,3072]{1,0:T(8,128)(2,1)} %get-tuple-element.37) | copy-start | bytes 1179652
  317.0 15.0 %copy-start.3 = (f32[1,3072]{1,0:T(1,128)S(1)}, f32[1,3072]{1,0:T(1,128)}, u32[]{:S(2)}) copy-start(f32[1,3072]{1,0:T(1,128)} %get-tuple-element.17) | copy-start | bytes 36868
Sparse Core Ops, SparseCore 0:
  24.7 30.5 all-gather.4
  57.2 32.3 all-gather.6
